TPU v7x, 32 devices: a whole 2x2x4 slice. The times are simulated.
32 devices in a mesh: blk: 8 (over z, y), inner: 4 (over x, core).
Axes of the slice: x: 2, y: 2, z: 4, core: 2. Of those that a mesh axis runs over, the one named last changes fastest.
Arguments:
- query_emb: bfloat16 [320, 1536], P(('blk', 'inner')), may hold values from -2 to 2, as said below
- doc_emb: bfloat16 [320, 1536], P(('blk', 'inner')), may hold values from -2 to 2, as said below
- positive: int32 [320], P(('blk', 'inner')), may hold values from 0 to 319, each once
- query_source: int32 [320], P(('blk', 'inner')), may hold values from 0 to 39
- doc_source: int32 [320], P(('blk', 'inner')), may hold values from 0 to 39
Outputs:
- row_loss: float32 [320], P(('blk', 'inner'))
- grad_query: float32 [320, 1536], P(('blk', 'inner'))
- grad_doc: float32 [320, 1536], P(('blk', 'inner'))
Inputs may be any that keep to these rules, and one draw needn't show every extreme that they name: `query_emb`: real embeddings of order 1536 ** -0.5 per entry. `doc_emb`: real embeddings of order 1536 ** -0.5 per entry.
All inputs are finite; a program needn't handle non-finite values.
Results may differ from a plain program's by a relative error of at most 0.005.
Values may be sent and summed in bfloat16 or wider, within the bound.
A program may use at most 64 MiB of HBM per device.

v0:
```python
import jax
import jax.numpy as jnp
from jax import lax
from jax.sharding import PartitionSpec as P

EPS = 1e-06
INV_TAU = 100.0
NEG = -1e30


def joined_2(value, axis, join):
    pieces = jax.tree.map(lambda part: lax.all_gather(part, axis), value)
    head = jax.tree.map(lambda part: part[0], pieces)
    tail = jax.tree.map(lambda part: part[1:], pieces)
    so_far, _ = lax.scan(lambda so_far, piece: (join(so_far, piece), None), head, tail)
    return so_far


def unit_rows(values):
    widened = values.astype(jnp.float32)
    lengths = jnp.sqrt(jnp.sum(widened * widened, axis=1, keepdims=True) + EPS)
    return (widened / lengths, lengths)


def scaled_gram(left_rows, right_rows):
    return (
        lax.dot_general(
            left_rows, right_rows, (((1,), (1,)), ((), ())), preferred_element_type=jnp.float32
        )
        * INV_TAU
    )


def pair_masks(row_info, col_info):
    row_qsource, row_dsource, row_target, row_global = row_info
    col_qsource, col_dsource, col_target, col_global = col_info
    mask_qd = (col_global[None, :] == row_target[:, None]) | (
        col_dsource[None, :] != row_qsource[:, None]
    )
    mask_dq = (col_target[None, :] != row_global[:, None]) & (
        col_qsource[None, :] != row_dsource[:, None]
    )
    mask_qq = col_qsource[None, :] != row_qsource[:, None]
    mask_dd = col_dsource[None, :] != row_dsource[:, None]
    twin_dq = (row_target[:, None] != col_global[None, :]) & (
        row_qsource[:, None] != col_dsource[None, :]
    )
    twin_qd = (row_global[:, None] == col_target[None, :]) | (
        row_dsource[:, None] != col_qsource[None, :]
    )
    return (mask_qd, mask_dq, mask_qq, mask_dd, twin_dq, twin_qd)


def masked_terms(scores_list, masks_list):
    peak = jnp.max(jnp.where(masks_list[0], scores_list[0], NEG), axis=1)
    for scores, masked in zip(scores_list[1:], masks_list[1:]):
        peak = jnp.maximum(peak, jnp.max(jnp.where(masked, scores, NEG), axis=1))
    totals = jnp.zeros(peak.shape, jnp.float32)
    for scores, masked in zip(scores_list, masks_list):
        totals = totals + jnp.sum(jnp.exp(jnp.where(masked, scores - peak[:, None], NEG)), axis=1)
    return (peak, totals)


def joined(former, latter):
    peak = jnp.maximum(former[0], latter[0])
    return (peak, former[1] * jnp.exp(former[0] - peak) + latter[1] * jnp.exp(latter[0] - peak))


def merge_stats(former, latter):
    query_pair = joined((former[0], former[1]), (latter[0], latter[1]))
    doc_pair = joined((former[2], former[3]), (latter[2], latter[3]))
    return (query_pair[0], query_pair[1], doc_pair[0], doc_pair[1], former[4] + latter[4])


def column_global(offset, amount, rows_dev, inner_count, inner_pos):
    flat = offset + jnp.arange(amount, dtype=jnp.int32)
    return flat // rows_dev * (inner_count * rows_dev) + inner_pos * rows_dev + flat % rows_dev


def weight(masked, scores, norms):
    return jnp.exp(jnp.where(masked, scores - norms, NEG))


def weighted(weights, right_rows):
    return jnp.dot(weights.astype(jnp.bfloat16), right_rows, preferred_element_type=jnp.float32)


def shards(query_emb, doc_emb, positive, query_source, doc_source):
    rows_dev = query_emb.shape[0]
    inner_count = lax.axis_size("inner")
    inner_pos = lax.axis_index("inner")
    blk_pos = lax.axis_index("blk")
    group_base = blk_pos * inner_count * rows_dev
    unit_query, query_len = unit_rows(query_emb)
    unit_doc, doc_len = unit_rows(doc_emb)
    query_half = unit_query.astype(jnp.bfloat16)
    doc_half = unit_doc.astype(jnp.bfloat16)
    row_query, row_doc, row_qsource, row_dsource, row_target = (
        lax.all_gather(query_half, "inner", axis=0, tiled=True),
        lax.all_gather(doc_half, "inner", axis=0, tiled=True),
        lax.all_gather(query_source, "inner", axis=0, tiled=True),
        lax.all_gather(doc_source, "inner", axis=0, tiled=True),
        lax.all_gather(positive, "inner", axis=0, tiled=True),
    )
    row_global = group_base + jnp.arange(row_query.shape[0], dtype=jnp.int32)
    own_start = inner_pos * rows_dev

    def col_index(offset, amount):
        return column_global(offset, amount, rows_dev, inner_count, inner_pos)

    row_count = row_query.shape[0]
    row_info = (row_qsource, row_dsource, row_target, row_global)

    def tile(pieces, offset):
        col_query, col_doc, col_qsource, col_dsource, col_target = pieces
        col_global = col_index(offset, col_query.shape[0])
        scores = (
            scaled_gram(row_query, col_doc),
            scaled_gram(row_doc, col_query),
            scaled_gram(row_query, col_query),
            scaled_gram(row_doc, col_doc),
        )
        masks = pair_masks(row_info, (col_qsource, col_dsource, col_target, col_global))
        return (col_global, scores, masks)

    empty_peak = jnp.full((row_count,), NEG, jnp.float32)
    empty_sum = jnp.zeros((row_count,), jnp.float32)
    start_stats = (empty_peak, empty_sum, empty_peak, empty_sum, empty_sum)
    columns = (
        lax.all_gather(query_half, "blk", axis=0, tiled=True),
        lax.all_gather(doc_half, "blk", axis=0, tiled=True),
        lax.all_gather(query_source, "blk", axis=0, tiled=True),
        lax.all_gather(doc_source, "blk", axis=0, tiled=True),
        lax.all_gather(positive, "blk", axis=0, tiled=True),
    )
    col_global, scores, masks = tile(columns, 0)
    query_side = masked_terms([scores[0], scores[2]], [masks[0], masks[2]])
    doc_side = masked_terms([scores[1], scores[3]], [masks[1], masks[3]])
    hit = jnp.sum(jnp.where(col_global[None, :] == row_target[:, None], scores[0], 0.0), axis=1)
    stats = merge_stats(start_stats, (query_side[0], query_side[1], doc_side[0], doc_side[1], hit))
    stats = joined_2(stats, "inner", merge_stats)
    query_lse = stats[0] + jnp.log(stats[1])
    doc_lse = stats[2] + jnp.log(stats[3])
    own_doc_lse = lax.dynamic_slice_in_dim(doc_lse, own_start, rows_dev, 0)
    doc_lse_all, target_all = (
        lax.all_gather(own_doc_lse, ("blk", "inner"), axis=0, tiled=True),
        lax.all_gather(positive, ("blk", "inner"), axis=0, tiled=True),
    )
    own_query_lse = lax.dynamic_slice_in_dim(query_lse, own_start, rows_dev, 0)
    own_hit = lax.dynamic_slice_in_dim(stats[4], own_start, rows_dev, 0)
    own_norm = jnp.logaddexp(own_query_lse, jnp.take(doc_lse_all, positive))
    row_loss = own_norm - own_hit
    norm_all = lax.all_gather(own_norm, ("blk", "inner"), axis=0, tiled=True)
    pairs = norm_all.shape[0]
    inverse = jnp.zeros((pairs,), jnp.int32).at[target_all].set(jnp.arange(pairs, dtype=jnp.int32))
    doc_norm_all = jnp.take(norm_all, inverse)
    row_norm = jnp.take(norm_all, row_global)[:, None]
    row_doc_norm = jnp.take(doc_norm_all, row_global)[:, None]
    col_global, scores, masks = tile(columns, 0)
    col_query = columns[0]
    col_doc = columns[1]
    col_target = columns[4]
    col_norm = jnp.take(norm_all, col_global)[None, :]
    col_doc_norm = jnp.take(doc_norm_all, col_global)[None, :]
    qd_weight = (
        weight(masks[0], scores[0], row_norm)
        + weight(masks[4], scores[0], col_doc_norm)
        - (col_global[None, :] == row_target[:, None]).astype(jnp.float32)
    )
    qq_weight = weight(masks[2], scores[2], row_norm) + weight(masks[2], scores[2], col_norm)
    dq_weight = (
        weight(masks[1], scores[1], row_doc_norm)
        + weight(masks[5], scores[1], col_norm)
        - (col_target[None, :] == row_global[:, None]).astype(jnp.float32)
    )
    dd_weight = weight(masks[3], scores[3], row_doc_norm) + weight(
        masks[3], scores[3], col_doc_norm
    )
    query_grad = (weighted(qd_weight, col_doc) + weighted(qq_weight, col_query)) * INV_TAU
    doc_grad = (weighted(dq_weight, col_query) + weighted(dd_weight, col_doc)) * INV_TAU
    query_part, doc_part = (
        lax.psum_scatter(query_grad, "inner", scatter_dimension=0, tiled=True),
        lax.psum_scatter(doc_grad, "inner", scatter_dimension=0, tiled=True),
    )
    grad_query = (
        query_part - unit_query * jnp.sum(unit_query * query_part, axis=1, keepdims=True)
    ) / query_len
    grad_doc = (doc_part - unit_doc * jnp.sum(unit_doc * doc_part, axis=1, keepdims=True)) / doc_len
    return (row_loss, grad_query, grad_doc)


def solution(mesh):
    placed = (
        P(("blk", "inner"), None),
        P(("blk", "inner"), None),
        P(("blk", "inner")),
        P(("blk", "inner")),
        P(("blk", "inner")),
    )
    return jax.shard_map(
        shards,
        mesh=mesh,
        in_specs=placed,
        out_specs=(P(("blk", "inner")), P(("blk", "inner"), None), P(("blk", "inner"), None)),
        check_vma=False,
    )
```

profile of v0, /device:TPU:1, one launch (start us, length us, event | category | flops | bytes accessed | tf_op | source)
XLA Modules:
  0.0 314.4 jit_solution(10777245465056686817)
XLA Ops:
  7.2 0.9 fusion.15
  8.3 6.7 %all-gather.6 = bf16[4,10,1536]{2,1,0:T(8,128)(2,1)S(1)} all-gather(bf16[1,10,1536]{2,1,0:T(8,128)(2,1)S(1)} %convert_bitcast_fusion), channel_id=1, replica_groups=mesh['blk'=8,'inner'=4] {'inner'}, dimensions={0}, use_global_device_ids=true | all-gather | bytes 153600 | tf_op jit(solution)/shard_map/all_gather | solution.py:100
  15.0 25.6 %all-gather.2 = bf16[8,10,1536]{2,1,0:T(8,128)(2,1)S(1)} all-gather(bf16[1,10,1536]{2,1,0:T(8,128)(2,1)S(1)} %convert_bitcast_fusion), channel_id=1, replica_groups=mesh['blk'=8,'inner'=4] {'blk'}, dimensions={0}, use_global_device_ids=true | all-gather | bytes 276480 | tf_op jit(solution)/shard_map/all_gather | solution.py:131
  40.8 25.0 %all-gather.3 = bf16[8,10,1536]{2,1,0:T(8,128)(2,1)S(1)} all-gather(bf16[1,10,1536]{2,1,0:T(8,128)(2,1)S(1)} %convert_bitcast_fusion.1), channel_id=1, replica_groups=mesh['blk'=8,'inner'=4] {'blk'}, dimensions={0}, use_global_device_ids=true | all-gather | bytes 276480 | tf_op jit(solution)/shard_map/all_gather | solution.py:130
  65.8 17.9 %all-gather.1 = bf16[4,10,1536]{2,1,0:T(8,128)(2,1)S(1)} all-gather(bf16[1,10,1536]{2,1,0:T(8,128)(2,1)S(1)} %convert_bitcast_fusion.1), channel_id=1, replica_groups=mesh['blk'=8,'inner'=4] {'inner'}, dimensions={0}, use_global_device_ids=true | all-gather | bytes 153600 | tf_op jit(solution)/shard_map/all_gather | solution.py:99
  83.6 0.7 copy-done.12
  91.4 4.1 %all-reduce.13 = (s32[40]{0:T(128)S(1)}, s32[40]{0:T(128)S(1)}, s32[40]{0:T(128)S(1)}) all-reduce(s32[40]{0:T(128)S(1)} %dynamic-update-slice.5, s32[40]{0:T(128)S(1)} %dynamic-update-slice.2, s32[40]{0:T(128)S(1)} %dynamic-update-slice), channel_id=1, replica_groups=mesh['blk'=8,'inner'=4] {'inner'}, use_global_device_ids=true, to_apply=%add.5 | all-reduce | flops 120 | bytes 960
  95.5 8.1 %all-reduce.12 = (s32[80]{0:T(128)S(1)}, s32[80]{0:T(128)S(1)}, s32[80]{0:T(128)S(1)}) all-reduce(s32[80]{0:T(128)S(1)} %dynamic-update-slice.1, s32[80]{0:T(128)S(1)} %dynamic-update-slice.3, s32[80]{0:T(128)S(1)} %dynamic-update-slice.4), channel_id=1, replica_groups=mesh['blk'=8,'inner'=4] {'blk'}, use_global_device_ids=true, to_apply=%add.1 | all-reduce | flops 240 | bytes 1920
  104.8 8.6 %all-reduce.6 = f32[160]{0:T(256)S(1)} all-reduce(f32[160]{0:T(256)S(1)} %dynamic-update-slice.6), channel_id=2, replica_groups=mesh['blk'=8,'inner'=4] {'inner'}, use_global_device_ids=true, to_apply=%add.6 | all-reduce | flops 160 | bytes 1280
  113.9 5.5 %all-gather.8 = f32[4,1,40]{2,1,0:T(1,128)S(1)} all-gather(f32[1,1,40]{2,1,0:T(1,128)S(1)} %fusion.68), channel_id=1, replica_groups=mesh['blk'=8,'inner'=4] {'inner'}, dimensions={0}, use_global_device_ids=true | all-gather | bytes 800 | tf_op jit(solution)/shard_map/all_gather | solution.py:12
  120.0 5.0 %all-gather.5 = f32[4,1,40]{2,1,0:T(1,128)S(1)} all-gather(f32[1,1,40]{2,1,0:T(1,128)S(1)} %fusion.71), channel_id=1, replica_groups=mesh['blk'=8,'inner'=4] {'inner'}, dimensions={0}, use_global_device_ids=true | all-gather | bytes 800 | tf_op jit(solution)/shard_map/all_gather | solution.py:12
  125.6 5.0 %all-gather.4 = f32[4,1,40]{2,1,0:T(1,128)S(1)} all-gather(f32[1,1,40]{2,1,0:T(1,128)S(1)} %get-tuple-element.118), channel_id=1, replica_groups=mesh['blk'=8,'inner'=4] {'inner'}, dimensions={0}, use_global_device_ids=true | all-gather | bytes 800 | tf_op jit(solution)/shard_map/all_gather | solution.py:12
  131.2 5.0 %all-gather.7 = f32[4,1,40]{2,1,0:T(1,128)S(1)} all-gather(f32[1,1,40]{2,1,0:T(1,128)S(1)} %get-tuple-element.116), channel_id=1, replica_groups=mesh['blk'=8,'inner'=4] {'inner'}, dimensions={0}, use_global_device_ids=true | all-gather | bytes 800 | tf_op jit(solution)/shard_map/all_gather | solution.py:12
  137.6 0.7 slice-done.2
  138.2 0.7 slice-done.3
  138.9 0.7 slice-done.4
  140.6 36.4 %all-reduce.7 = f32[320]{0:T(512)S(1)} all-reduce(f32[320]{0:T(512)S(1)} %dynamic-slice_dynamic-update-slice_fusion), channel_id=1, replica_groups=mesh['blk'=8,'inner'=4] {'blk','inner'}, use_global_device_ids=true, to_apply=%add.7 | all-reduce | flops 320 | bytes 2560
  177.0 0.7 gather_fusion
  177.9 42.0 %all-reduce.8 = f32[320]{0:T(512)S(1)} all-reduce(f32[320]{0:T(512)S(1)} %get-tuple-element.114), channel_id=1, replica_groups=mesh['blk'=8,'inner'=4] {'blk','inner'}, use_global_device_ids=true, to_apply=%add.8 | all-reduce | flops 320 | bytes 2560
  220.0 38.7 %all-reduce.9 = s32[320]{0:T(512)S(1)} all-reduce(s32[320]{0:T(512)S(1)} %dynamic-update-slice.9), channel_id=1, replica_groups=mesh['blk'=8,'inner'=4] {'blk','inner'}, use_global_device_ids=true, to_apply=%add.9 | all-reduce | flops 320 | bytes 2560
  258.8 2.9 scatter_custom_fusion
  261.7 2.4 gather_fusion.1
  264.2 0.8 gather_fusion.2
  265.0 0.8 gather_fusion.5
  265.8 1.3 gather_fusion.3
  267.1 1.3 gather_fusion.4
  268.6 1.0 fusion.12
  269.8 1.0 fusion.13
  272.1 31.7 %all-reduce.17.cloned.1.call-done = (f32[40,1536]{1,0:T(8,128)}, f32[40,1536]{1,0:T(8,128)}) async-done(((f32[40,1536]{1,0:T(8,128)}, f32[40,1536]{1,0:T(8,128)}), (f32[40,1536]{1,0:T(8,128)}, f32[40,1536]{1,0:T(8,128)})) %all-reduce.17.cloned.1.call-update) | async-done | bytes 491536
  303.8 1.1 multiply_reduce_fusion
  304.9 1.6 subtract_divide_fusion
  306.8 0.7 subtract_divide_fusion.1
  (112 shorter events, 13.0 us)
Async XLA Ops:
  7.2 1.0 copy-start
  7.2 296.6 %all-reduce.17.cloned.1.call-start = ((), (), s32[]{:S(2)}) async-start(), calls=%async_computation | async-start | bytes 983040
  15.0 25.6 %copy-start.1 = (bf16[10,1536]{1,0:T(8,128)(2,1)S(1)}, bf16[10,1536]{1,0:T(8,128)(2,1)}, u32[]{:S(2)}) copy-start(bf16[10,1536]{1,0:T(8,128)(2,1)} %param.11) | copy-start | bytes 92164
  83.6 0.7 copy-start.12
  84.3 0.7 copy-start.8
  86.9 0.7 copy-start.11
  87.8 0.7 copy-start.10
  89.0 0.7 copy-start.9
  113.4 0.6 copy-start.3
  119.4 0.6 copy-start.4
  125.0 0.6 copy-start.5
  130.7 0.6 copy-start.6
  136.3 0.6 copy-start.7
  136.9 0.7 slice-start.1
  137.6 0.7 slice-start.2
  138.2 0.7 slice-start.3
  138.9 0.7 slice-start.4
  139.6 0.6 slice-start
  303.8 2.8 copy-start.2
Sparse Core Ops, SparseCore 0:
  270.9 32.8 all-reduce.16
where the time goes:
time: 317 us; the launch traced here: 314 us
  blocking collectives  234 us (74%)
  waiting for transfers between devices  31.7 us (10%)
  local copies, waits for them, and re-layouts  22.3 us (7%)
  between operations  16.9 us (5%)
  other arithmetic  6.25 us (2%)
  matrix products  3.4 us (1%)
    unnamed x6, blocking collectives  138 us
    unnamed x2, waiting for transfers between devices  31.7 us
    all_gather x1, blocking collectives, shards(): lax.all_gather(doc_half, 'blk', axis=0, tiled=True)  25.6 us
    all_gather x1, blocking collectives, shards(): lax.all_gather(query_half, 'blk', axis=0, tiled=True)  25 us
    all_gather x4, blocking collectives, joined_2(): pieces = jax.tree.map(lambda part: lax.all_gather(part, axis), value)  20.6 us
    all_gather x1, blocking collectives, shards(): lax.all_gather(query_half, 'inner', axis=0, tiled=True)  17.9 us
    unnamed x51, local copies, waits for them, and re-layouts  8.79 us
    all_gather x1, blocking collectives, shards(): lax.all_gather(doc_half, 'inner', axis=0, tiled=True)  6.73 us
  transfers between devices with their start and end apart: 1, of which 1 were waited for; matrix products, arithmetic and copies ran while one was open for 0% of the time, Pallas kernels for 0%

commit v1 on v0

--- a/solution.py
+++ b/solution.py
@@ -1,6 +1,10 @@
+import functools
+
 import jax
 import jax.numpy as jnp
 from jax import lax
+from jax.experimental import pallas as pl
+from jax.experimental.pallas import tpu as pltpu
 from jax.sharding import PartitionSpec as P
 
 EPS = 1e-06
@@ -189,7 +193,288 @@
     return (row_loss, grad_query, grad_doc)
 
 
+def gather_kernel(
+    depth, q_ref, d_ref, pos_ref, qs_ref, ds_ref, loss_ref, gq_ref, gd_ref,
+    buf, rows_all, unit_own, len_own, scol, ucol, srow, urow, lse_self, lse_pair, send_sem, recv_sem,
+):
+    f32, bf16 = jnp.float32, jnp.bfloat16
+    rows = q_ref.shape[0]
+    width = q_ref.shape[1]
+    quarter = width // 4
+    blk, inner = lax.axis_index("blk"), lax.axis_index("inner")
+    z, y = blk // 2, blk % 2
+    x, core = inner // 2, inner % 2
+    me = blk * 4 + inner
+
+    def place(zz, flip_a, flip_b):
+        flip_y = flip_a * (1 - core) + flip_b * core
+        flip_x = flip_a * core + flip_b * (1 - core)
+        yy = y + flip_y * (1 - 2 * y)
+        xx = x + flip_x * (1 - 2 * x)
+        return zz * 2 + yy, xx * 2 + core
+
+    def slot_of(zz, flip_a, flip_b):
+        b, i = place(zz, flip_a, flip_b)
+        return b * 4 + i
+
+    peer_a = place(z, 1, 0)
+    peer_b = place(z, 0, 1)
+    peer_core = (blk, x * 2 + 1 - core)
+    peer_up = (blk + 2, inner)
+    peer_down = (blk - 2, inner)
+
+    barrier = pltpu.get_barrier_semaphore()
+
+    def greet(peer):
+        pl.semaphore_signal(barrier, inc=1, device_id=peer, device_id_type=pl.DeviceIdType.MESH)
+
+    greet(peer_a)
+    greet(peer_b)
+    greet(peer_core)
+
+    @pl.when(z < depth - 1)
+    def _():
+        greet(peer_up)
+
+    @pl.when(z > 0)
+    def _():
+        greet(peer_down)
+
+    unit_own[...] = jnp.zeros_like(unit_own)
+    len_own[...] = jnp.ones_like(len_own)
+    for ref, first in ((q_ref, 0), (d_ref, 16)):
+        wide = ref[...].astype(f32)
+        lengths = jnp.sqrt(jnp.sum(wide * wide, axis=1, keepdims=True) + EPS)
+        unit_own[pl.ds(first, rows), :] = wide / lengths
+        len_own[pl.ds(first, rows), :] = jnp.broadcast_to(lengths, (rows, 128))
+    own = unit_own[...].astype(bf16)
+
+    row = lax.broadcasted_iota(jnp.int32, (32, 128), 0)
+    lane = lax.broadcasted_iota(jnp.int32, (32, 128), 1)
+    source = jnp.zeros((32, 128), jnp.int32)
+    key = jnp.zeros((32, 128), jnp.int32)
+    for r in range(rows):
+        source = jnp.where(row == r, qs_ref[r], source)
+        source = jnp.where(row == 16 + r, ds_ref[r], source)
+        key = jnp.where(row == r, pos_ref[r], key)
+    key = jnp.where(row >= 16, me * rows + row - 16, key)
+    kind = jnp.where(row >= 16, 0.25, 0.0).astype(f32)
+    valid = (row % 16) < rows
+    own_source = source.astype(f32)
+    own_key = jnp.where(valid, key.astype(f32) + kind, -100.0)
+    parts = (
+        (source >> 5).astype(f32),
+        (source & 31).astype(f32),
+        (key >> 5).astype(f32),
+        (key & 31).astype(f32) + kind,
+    )
+
+    def lanes(first):
+        out = jnp.zeros((32, 128), f32)
+        for k, part in enumerate(parts):
+            out = jnp.where(lane == first + k, part, out)
+        return out.astype(bf16)
+
+    def select(shape, chosen):
+        r = lax.broadcasted_iota(jnp.int32, shape, 0)
+        c = lax.broadcasted_iota(jnp.int32, shape, 1)
+        return chosen(r, c).astype(f32).astype(bf16)
+
+    def mm(a, b):
+        return jnp.dot(a, b, preferred_element_type=f32)
+
+    def mmt(a, b):
+        return lax.dot_general(a, b, (((1,), (1,)), ((), ())), preferred_element_type=f32)
+
+    head = select((16, 32), lambda r, c: c == jnp.where(r < rows, r, r + 16 - rows))
+    rest = [
+        select((16, 32), lambda r, c, k=k: (r // 4 == k) & (c == 32 - rows + r % 4)) for k in range(4)
+    ]
+    mine = pl.ds(pl.multiple_of(me * 16, 16), 16)
+    buf[mine, 0:width] = mm(head, own).astype(bf16)
+    tail = mm(rest[0], own[:, 0:quarter])
+    for k in range(1, 4):
+        tail = tail + mm(rest[k], own[:, k * quarter : (k + 1) * quarter])
+    buf[mine, width : width + quarter] = tail.astype(bf16)
+    buf[mine, width + quarter :] = (mm(head, lanes(0)) + mm(rest[0], lanes(4))).astype(bf16)
+
+    pl.semaphore_wait(barrier, 3 + jnp.minimum(z, 1) + jnp.minimum(depth - 1 - z, 1))
+
+    def copy(slot, sem, peer):
+        piece = buf.at[pl.ds(pl.multiple_of(slot * 16, 16), 16)]
+        return pltpu.make_async_remote_copy(
+            src_ref=piece, dst_ref=piece, send_sem=send_sem.at[sem], recv_sem=recv_sem.at[slot],
+            device_id=peer, device_id_type=pl.DeviceIdType.MESH,
+        )
+
+    def sends(zz, flip_a, flip_b):
+        slot = slot_of(zz, flip_a, flip_b)
+        out = []
+        if not flip_a and not flip_b:
+            out.append((copy(slot, zz, peer_up), (zz <= z) & (z < depth - 1)))
+            out.append((copy(slot, depth + zz, peer_down), (zz >= z) & (z > 0)))
+            out.append((copy(slot, 2 * depth + zz, peer_a), None))
+        if not flip_b:
+            out.append((copy(slot, (3 + flip_a) * depth + zz, peer_b), None))
+        out.append((copy(slot, (5 + 2 * flip_b + flip_a) * depth + zz, peer_core), None))
+        return out
+
+    def each(copies, act):
+        for one, under in copies:
+            if under is None:
+                act(one)
+            else:
+                pl.when(under)(functools.partial(act, one))
+
+    def start(one):
+        one.start()
+
+    def arrive(slot):
+        copy(slot, 0, peer_core).wait_recv()
+
+    def handle(dist, flip_a, flip_b):
+        def at(zz):
+            if dist or flip_a or flip_b:
+                arrive(slot_of(zz, flip_a, flip_b))
+            each(sends(zz, flip_a, flip_b), start)
+
+        if dist == 0:
+            at(z)
+        else:
+            pl.when(z - dist >= 0)(lambda: at(z - dist))
+            pl.when(z + dist < depth)(lambda: at(z + dist))
+
+    order = sorted(
+        ((dist + a + b, a + b, dist, a, b) for dist in range(depth) for a in (0, 1) for b in (0, 1))
+    )
+    for _, _, dist, a, b in order:
+        handle(dist, a, b)
+
+    def from_core(zz, carry):
+        for fb in (0, 1):
+            for fa in (0, 1):
+                s = slot_of(zz, fa, fb)
+                arrive(s + 1 - 2 * core)
+        return carry
+
+    lax.fori_loop(0, depth, from_core, 0)
+
+    count = 2 * rows * buf.shape[0] // 16
+    heads = buf.shape[0]
+    tails = count - heads
+    rows_all[0:heads, :] = buf[:, 0:width]
+    left = buf[:, width : width + quarter]
+    meta = buf[:, width + quarter :]
+    picks = [
+        select((tails, heads), lambda r, c, k=k: c == r // 4 * 16 + k * 4 + r % 4) for k in range(4)
+    ]
+    for k in range(4):
+        rows_all[heads:, k * quarter : (k + 1) * quarter] = mm(picks[k], left).astype(bf16)
+    meta_tail = mm(picks[0], meta).astype(bf16)
+
+    def reader(first, axis, shape):
+        pos = lax.broadcasted_iota(jnp.int32, shape, axis)
+        return jnp.where(pos == first, 32.0, jnp.where(pos == first + 1, 1.0, 0.0)).astype(bf16)
+
+    for ref, first in ((scol, 0), (ucol, 2)):
+        ref[0:heads, :] = mm(meta, reader(first, 0, (128, 128)))
+        ref[heads:, :] = mm(meta_tail, reader(first + 4, 0, (128, 128)))
+    for ref, first in ((srow, 0), (urow, 2)):
+        ref[:, 0:heads] = mmt(reader(first, 1, (8, 128)), meta)
+        ref[:, heads:] = mmt(reader(first + 4, 1, (8, 128)), meta_tail)
+    s_row, u_row = srow[0:1, :], urow[0:1, :]
+    lse_self[...] = jnp.zeros_like(lse_self)
+    lse_pair[...] = jnp.zeros_like(lse_pair)
+    chunk = 128
+
+    def forward(step, carry):
+        at = pl.ds(pl.multiple_of(step * chunk, chunk), chunk)
+        scores = mmt(rows_all[at, :], rows_all[...]) * INV_TAU
+        apart = u_row - ucol[at, 0:1]
+        allowed = (apart == 0.25) | ((s_row != scol[at, 0:1]) & (apart != -0.25))
+        scores = jnp.where(allowed, scores, NEG)
+        peak = jnp.max(scores, axis=1, keepdims=True)
+        total = jnp.sum(jnp.exp(scores - peak), axis=1, keepdims=True)
+        lse = jnp.where(peak > 0.5 * NEG, peak + jnp.log(total), NEG)
+        lse_self[0:1, :] += jnp.sum(jnp.where(apart == 0.0, lse, 0.0), axis=0, keepdims=True)
+        lse_pair[0:1, :] += jnp.sum(
+            jnp.where(jnp.abs(apart) == 0.25, lse, 0.0), axis=0, keepdims=True
+        )
+        return carry
+
+    lax.fori_loop(0, count // chunk, forward, 0)
+    first, second = lse_self[0:1, :], lse_pair[0:1, :]
+    norm_row = jnp.maximum(first, second) + jnp.log(1.0 + jnp.exp(-jnp.abs(first - second)))
+
+    scores = mmt(own, rows_all[...]) * INV_TAU
+    apart = u_row - own_key[:, 0:1]
+    hit = jnp.abs(apart) == 0.25
+    norm_own = jnp.sum(jnp.where(apart == 0.0, norm_row, 0.0), axis=1, keepdims=True)
+    loss = norm_own - jnp.sum(jnp.where(hit, scores, 0.0), axis=1, keepdims=True)
+    loss_ref[...] = jnp.broadcast_to(loss, loss_ref.shape)
+    from_own = jnp.exp(scores - norm_own)
+    apart_source = (s_row != own_source[:, 0:1]) & (own_key[:, 0:1] >= 0.0)
+    weights = jnp.where(
+        hit, from_own - 1.0, jnp.where(apart_source, from_own + jnp.exp(scores - norm_row), 0.0)
+    )
+    grads = mm(weights.astype(bf16), rows_all[...]) * INV_TAU
+    unit = unit_own[...]
+    grads = (grads - unit * jnp.sum(unit * grads, axis=1, keepdims=True)) / len_own[:, 0:1]
+    gq_ref[...] = grads[0:rows, :]
+    gd_ref[...] = grads[16 : 16 + rows, :]
+
+    def done(one):
+        one.wait_send()
+
+    def finish(zz, carry):
+        for fa in (0, 1):
+            for fb in (0, 1):
+                each(sends(zz, fa, fb), done)
+        return carry
+
+    lax.fori_loop(0, depth, finish, 0)
+
+
+def whole_batch(depth, query_emb, doc_emb, positive, query_source, doc_source):
+    rows, width = query_emb.shape
+    devices = lax.axis_size("blk") * lax.axis_size("inner")
+    count = 2 * rows * devices
+    vmem = pl.BlockSpec(memory_space=pltpu.VMEM)
+    smem = pl.BlockSpec(memory_space=pltpu.SMEM)
+    f32 = jnp.float32
+    loss, grad_query, grad_doc = pl.pallas_call(
+        functools.partial(gather_kernel, depth),
+        out_shape=(
+            jax.ShapeDtypeStruct((32, 128), f32),
+            jax.ShapeDtypeStruct((rows, width), f32),
+            jax.ShapeDtypeStruct((rows, width), f32),
+        ),
+        in_specs=[vmem, vmem, smem, smem, smem],
+        out_specs=(vmem, vmem, vmem),
+        scratch_shapes=[
+            pltpu.VMEM((devices * 16, width + width // 4 + 128), jnp.bfloat16),
+            pltpu.VMEM((count, width), jnp.bfloat16),
+            pltpu.VMEM((32, width), f32),
+            pltpu.VMEM((32, 128), f32),
+            pltpu.VMEM((count, 128), f32),
+            pltpu.VMEM((count, 128), f32),
+            pltpu.VMEM((8, count), f32),
+            pltpu.VMEM((8, count), f32),
+            pltpu.VMEM((8, count), f32),
+            pltpu.VMEM((8, count), f32),
+            pltpu.SemaphoreType.DMA((9 * depth,)),
+            pltpu.SemaphoreType.DMA((devices,)),
+        ],
+        compiler_params=pltpu.CompilerParams(
+            collective_id=0, has_side_effects=True, vmem_limit_bytes=40 * 1024 * 1024
+        ),
+    )(query_emb, doc_emb, positive, query_source, doc_source)
+    return (loss[:rows, 0], grad_query, grad_doc)
+
+
 def solution(mesh):
+    small = mesh.shape["inner"] == 4 and mesh.shape["blk"] == 8
+    body = functools.partial(whole_batch, mesh.shape["blk"] // 2) if small else shards
     placed = (
         P(("blk", "inner"), None),
         P(("blk", "inner"), None),
@@ -198,7 +483,7 @@
         P(("blk", "inner")),
     )
     return jax.shard_map(
-        shards,
+        body,
         mesh=mesh,
         in_specs=placed,
         out_specs=(P(("blk", "inner")), P(("blk", "inner"), None), P(("blk", "inner"), None)),

time: 317 us -> 36.7 us (0.12)
  blocking collectives: 234 us -> 0 us
  waiting for transfers between devices: 31.7 us -> 0 us
  Pallas kernels: 0 us -> 30.3 us
  local copies, waits for them, and re-layouts: 22.3 us -> 5.46 us
  between operations: 16.9 us -> 0.65 us
  other arithmetic: 6.25 us -> 0 us
  matrix products: 3.4 us -> 0 us
    unnamed x6 -> x0, blocking collectives: 138 us -> none
    all_gather x8 -> x0, blocking collectives: 95.7 us -> none  [the longest x1 25.6 us: shards(): lax.all_gather(doc_half, 'blk', axis=0, tiled=True)]
    unnamed x2 -> x0, waiting for transfers between devices: 31.7 us -> none
    pallas_call x0 -> x1, Pallas kernels: none -> 30.3 us  [whole_batch(): pl.pallas_call(functools.partial(gather_kernel, depth), out_shape=(jax.Sh...]
    gather x6 -> x0, local copies, waits for them, and re-layouts: 7.24 us -> none  [the longest x1 2.45 us: shards(): doc_norm_all = jnp.take(norm_all, inverse)]
    unnamed x51 -> x12, local copies, waits for them, and re-layouts: 8.79 us -> 4.83 us
    dot_general x8 -> x0, matrix products: 3.4 us -> none  [the longest x4 2.4 us: weighted(): jnp.dot(weights.astype(jnp.bfloat16), right_rows, preferred_element_type=...]
  transfers between devices with their start and end apart: 1 -> 0, of which waited for: 1 -> 0; matrix products, arithmetic and copies ran while one was open for 0% -> 0% of each run, Pallas kernels for 0% -> 0%
where the time goes in v1:
time: 36.7 us; the launch traced here: 36.4 us
  Pallas kernels  30.3 us (83%)
  local copies, waits for them, and re-layouts  5.46 us (15%)
  between operations  0.65 us (2%)
    pallas_call x1, Pallas kernels, whole_batch(): pl.pallas_call(functools.partial(gather_kernel, depth), out_shape=(jax.Sh...  30.3 us
    unnamed x12, local copies, waits for them, and re-layouts  4.83 us

profile of v1, /device:TPU:1, one launch (start us, length us, event | category | flops | bytes accessed | tf_op | source)
XLA Modules:
  0.0 36.4 jit_solution(438584477090210715)
XLA Ops:
  0.6 0.0 copy-start
  0.6 0.8 %copy-done = bf16[10,1536]{1,0:T(8,128)(2,1)S(1)} copy-done((bf16[10,1536]{1,0:T(8,128)(2,1)S(1)}, bf16[10,1536]{1,0:T(8,128)(2,1)}, u32[]{:S(2)}) %copy-start) | copy-done | bytes 30744
  1.4 0.0 copy-start.1
  1.4 0.8 %copy-done.1 = bf16[10,1536]{1,0:T(8,128)(2,1)S(1)} copy-done((bf16[10,1536]{1,0:T(8,128)(2,1)S(1)}, bf16[10,1536]{1,0:T(8,128)(2,1)}, u32[]{:S(2)}) %copy-start.1) | copy-done | bytes 30744
  2.2 0.0 copy-start.2
  2.2 0.7 %copy-done.2 = s32[10]{0:T(128)S(1)} copy-done((s32[10]{0:T(128)S(1)}, s32[10]{0:T(128)}, u32[]{:S(2)}) %copy-start.2) | copy-done | bytes 64
  2.9 0.0 copy-start.3
  2.9 0.7 %copy-done.3 = s32[10]{0:T(128)S(1)} copy-done((s32[10]{0:T(128)S(1)}, s32[10]{0:T(128)}, u32[]{:S(2)}) %copy-start.3) | copy-done | bytes 64
  3.5 0.0 copy-start.4
  3.5 0.7 %copy-done.4 = s32[10]{0:T(128)S(1)} copy-done((s32[10]{0:T(128)S(1)}, s32[10]{0:T(128)}, u32[]{:S(2)}) %copy-start.4) | copy-done | bytes 64
  4.2 30.3 %shard_map.76 = (f32[32,128]{1,0:T(8,128)S(1)}, f32[10,1536]{1,0:T(8,128)S(1)}, f32[10,1536]{1,0:T(8,128)S(1)}) custom-call(bf16[10,1536]{1,0:T(8,128)(2,1)S(1)} %copy-done, bf16[10,1536]{1,0:T(8,128)(2,1)S(1)} %copy-done.1, s32[10]{0:T(128)S(1)} %copy-done.2, s32[10]{0:T(128)S(1)} %copy-done.3, s32[10]{0:T(128)S(1)} %copy-done.4), custom_call_target="tpu_custom_call" | custom-call | tf_op jit(solution)/shard_map/pallas_call | solution.py:445
  34.5 0.6 %slice_reduce_fusion = f32[10]{0:T(128)} fusion(f32[32,128]{1,0:T(8,128)S(1)} %get-tuple-element.6), kind=kLoop, calls=%fused_computation | loop fusion | bytes 80 | tf_op jit(solution)/shard_map/slice | solution.py:472
  35.2 0.6 %copy.10 = f32[10,1536]{1,0:T(8,128)} copy(f32[10,1536]{1,0:T(8,128)S(1)} %get-tuple-element.13) | data formatting | bytes 122880
  35.8 0.6 %copy.11 = f32[10,1536]{1,0:T(8,128)} copy(f32[10,1536]{1,0:T(8,128)S(1)} %get-tuple-element.14) | data formatting | bytes 122880
Async XLA Ops:
  0.6 0.8 %copy-start = (bf16[10,1536]{1,0:T(8,128)(2,1)S(1)}, bf16[10,1536]{1,0:T(8,128)(2,1)}, u32[]{:S(2)}) copy-start(bf16[10,1536]{1,0:T(8,128)(2,1)} %q_ref.1) | copy-start | bytes 92164
  1.4 0.8 %copy-start.1 = (bf16[10,1536]{1,0:T(8,128)(2,1)S(1)}, bf16[10,1536]{1,0:T(8,128)(2,1)}, u32[]{:S(2)}) copy-start(bf16[10,1536]{1,0:T(8,128)(2,1)} %d_ref.1) | copy-start | bytes 92164
  2.2 0.7 %copy-start.2 = (s32[10]{0:T(128)S(1)}, s32[10]{0:T(128)}, u32[]{:S(2)}) copy-start(s32[10]{0:T(128)} %pos_ref.1) | copy-start | bytes 124
  2.9 0.7 %copy-start.3 = (s32[10]{0:T(128)S(1)}, s32[10]{0:T(128)}, u32[]{:S(2)}) copy-start(s32[10]{0:T(128)} %qs_ref.1) | copy-start | bytes 124
  3.5 0.7 %copy-start.4 = (s32[10]{0:T(128)S(1)}, s32[10]{0:T(128)}, u32[]{:S(2)}) copy-start(s32[10]{0:T(128)} %ds_ref.1) | copy-start | bytes 124

commit v2 on v1

--- a/solution.py
+++ b/solution.py
@@ -194,8 +194,8 @@
 
 
 def gather_kernel(
-    depth, q_ref, d_ref, pos_ref, qs_ref, ds_ref, loss_ref, gq_ref, gd_ref,
-    buf, rows_all, unit_own, len_own, scol, ucol, srow, urow, lse_self, lse_pair, send_sem, recv_sem,
+    depth, q_hbm, d_hbm, pos_hbm, qs_hbm, ds_hbm, loss_ref, gq_ref, gd_ref,
+    q_ref, d_ref, pos_ref, qs_ref, ds_ref, in_sem, buf, rows_all, unit_own, len_own, scol, ucol, srow, urow, lse_self, lse_pair, send_sem, recv_sem,
 ):
     f32, bf16 = jnp.float32, jnp.bfloat16
     rows = q_ref.shape[0]
@@ -219,27 +219,28 @@
 
     peer_a = place(z, 1, 0)
     peer_b = place(z, 0, 1)
+    peer_diag = place(z, 1, 1)
     peer_core = (blk, x * 2 + 1 - core)
-    peer_up = (blk + 2, inner)
-    peer_down = (blk - 2, inner)
+    upper = z // (depth // 2)
+    low = z * (1 - upper) + (depth - 1 - z) * upper
+
+    def near(k):
+        kth = k + jnp.minimum(jnp.maximum(k - low + 1, 0), 1)
+        return kth * (1 - upper) + (depth - 1 - kth) * upper
+
+    line = [near(k) for k in range(depth - 1)]
 
     barrier = pltpu.get_barrier_semaphore()
-
-    def greet(peer):
+    peers = [(zz * 2 + y, inner) for zz in line] + [peer_a, peer_b, peer_diag, peer_core]
+    for peer in peers:
         pl.semaphore_signal(barrier, inc=1, device_id=peer, device_id_type=pl.DeviceIdType.MESH)
 
-    greet(peer_a)
-    greet(peer_b)
-    greet(peer_core)
-
-    @pl.when(z < depth - 1)
-    def _():
-        greet(peer_up)
-
-    @pl.when(z > 0)
-    def _():
-        greet(peer_down)
-
+    held = ((q_hbm, q_ref), (d_hbm, d_ref), (pos_hbm, pos_ref), (qs_hbm, qs_ref), (ds_hbm, ds_ref))
+    loads = [pltpu.make_async_copy(a, b, in_sem.at[n]) for n, (a, b) in enumerate(held)]
+    for load in loads:
+        load.start()
+    for load in loads:
+        load.wait()
     unit_own[...] = jnp.zeros_like(unit_own)
     len_own[...] = jnp.ones_like(len_own)
     for ref, first in ((q_ref, 0), (d_ref, 16)):
@@ -298,7 +299,7 @@
     buf[mine, width : width + quarter] = tail.astype(bf16)
     buf[mine, width + quarter :] = (mm(head, lanes(0)) + mm(rest[0], lanes(4))).astype(bf16)
 
-    pl.semaphore_wait(barrier, 3 + jnp.minimum(z, 1) + jnp.minimum(depth - 1 - z, 1))
+    pl.semaphore_wait(barrier, len(peers))
 
     def copy(slot, sem, peer):
         piece = buf.at[pl.ds(pl.multiple_of(slot * 16, 16), 16)]
@@ -307,48 +308,32 @@
             device_id=peer, device_id_type=pl.DeviceIdType.MESH,
         )
 
-    def sends(zz, flip_a, flip_b):
-        slot = slot_of(zz, flip_a, flip_b)
+    def onward(k, flip_a, flip_b):
+        slot = slot_of(z if k == 0 else line[k - 1], flip_a, flip_b)
         out = []
         if not flip_a and not flip_b:
-            out.append((copy(slot, zz, peer_up), (zz <= z) & (z < depth - 1)))
-            out.append((copy(slot, depth + zz, peer_down), (zz >= z) & (z > 0)))
-            out.append((copy(slot, 2 * depth + zz, peer_a), None))
-        if not flip_b:
-            out.append((copy(slot, (3 + flip_a) * depth + zz, peer_b), None))
-        out.append((copy(slot, (5 + 2 * flip_b + flip_a) * depth + zz, peer_core), None))
-        return out
-
-    def each(copies, act):
-        for one, under in copies:
-            if under is None:
-                act(one)
-            else:
-                pl.when(under)(functools.partial(act, one))
-
-    def start(one):
-        one.start()
+            if k == 0:
+                for n, zz in enumerate(line):
+                    out.append(copy(slot, n, (zz * 2 + y, inner)))
+            out.append(copy(slot, depth + k, peer_a))
+            out.append(copy(slot, 2 * depth + k, peer_b))
+            out.append(copy(slot, 3 * depth + k, peer_diag))
+        out.append(copy(slot, (4 + 2 * flip_b + flip_a) * depth + k, peer_core))
+        return slot, out
 
     def arrive(slot):
         copy(slot, 0, peer_core).wait_recv()
 
-    def handle(dist, flip_a, flip_b):
-        def at(zz):
-            if dist or flip_a or flip_b:
-                arrive(slot_of(zz, flip_a, flip_b))
-            each(sends(zz, flip_a, flip_b), start)
-
-        if dist == 0:
-            at(z)
-        else:
-            pl.when(z - dist >= 0)(lambda: at(z - dist))
-            pl.when(z + dist < depth)(lambda: at(z + dist))
-
-    order = sorted(
-        ((dist + a + b, a + b, dist, a, b) for dist in range(depth) for a in (0, 1) for b in (0, 1))
-    )
-    for _, _, dist, a, b in order:
-        handle(dist, a, b)
+    order = sorted((k + (flip_a + flip_b), flip_a + flip_b, k, flip_a, flip_b)
+                   for k in range(depth) for flip_a in (0, 1) for flip_b in (0, 1))
+    started = []
+    for _, hops, k, flip_a, flip_b in order:
+        slot, copies = onward(k, flip_a, flip_b)
+        if k or hops:
+            arrive(slot)
+        for one in copies:
+            one.start()
+        started += copies
 
     def from_core(zz, carry):
         for fb in (0, 1):
@@ -385,7 +370,7 @@
     s_row, u_row = srow[0:1, :], urow[0:1, :]
     lse_self[...] = jnp.zeros_like(lse_self)
     lse_pair[...] = jnp.zeros_like(lse_pair)
-    chunk = 128
+    chunk = count
 
     def forward(step, carry):
         at = pl.ds(pl.multiple_of(step * chunk, chunk), chunk)
@@ -423,16 +408,8 @@
     gq_ref[...] = grads[0:rows, :]
     gd_ref[...] = grads[16 : 16 + rows, :]
 
-    def done(one):
+    for one in started:
         one.wait_send()
-
-    def finish(zz, carry):
-        for fa in (0, 1):
-            for fb in (0, 1):
-                each(sends(zz, fa, fb), done)
-        return carry
-
-    lax.fori_loop(0, depth, finish, 0)
 
 
 def whole_batch(depth, query_emb, doc_emb, positive, query_source, doc_source):
@@ -440,7 +417,6 @@
     devices = lax.axis_size("blk") * lax.axis_size("inner")
     count = 2 * rows * devices
     vmem = pl.BlockSpec(memory_space=pltpu.VMEM)
-    smem = pl.BlockSpec(memory_space=pltpu.SMEM)
     f32 = jnp.float32
     loss, grad_query, grad_doc = pl.pallas_call(
         functools.partial(gather_kernel, depth),
@@ -449,9 +425,15 @@
             jax.ShapeDtypeStruct((rows, width), f32),
             jax.ShapeDtypeStruct((rows, width), f32),
         ),
-        in_specs=[vmem, vmem, smem, smem, smem],
+        in_specs=[pl.BlockSpec(memory_space=pltpu.HBM)] * 5,
         out_specs=(vmem, vmem, vmem),
         scratch_shapes=[
+            pltpu.VMEM((rows, width), jnp.bfloat16),
+            pltpu.VMEM((rows, width), jnp.bfloat16),
+            pltpu.SMEM((rows,), jnp.int32),
+            pltpu.SMEM((rows,), jnp.int32),
+            pltpu.SMEM((rows,), jnp.int32),
+            pltpu.SemaphoreType.DMA((5,)),
             pltpu.VMEM((devices * 16, width + width // 4 + 128), jnp.bfloat16),
             pltpu.VMEM((count, width), jnp.bfloat16),
             pltpu.VMEM((32, width), f32),
@@ -462,7 +444,7 @@
             pltpu.VMEM((8, count), f32),
             pltpu.VMEM((8, count), f32),
             pltpu.VMEM((8, count), f32),
-            pltpu.SemaphoreType.DMA((9 * depth,)),
+            pltpu.SemaphoreType.DMA((8 * depth,)),
             pltpu.SemaphoreType.DMA((devices,)),
         ],
         compiler_params=pltpu.CompilerParams(

time: 36.7 us -> 31.6 us (0.86)
  Pallas kernels: 30.3 us -> 25.2 us
    pallas_call x1, Pallas kernels: 30.3 us -> 25.2 us  [whole_batch(): pl.pallas_call(functools.partial(gather_kernel, depth), out_shape=(jax.Sh...]
where the time goes in v2:
time: 31.6 us; the launch traced here: 31.3 us
  Pallas kernels  25.2 us (80%)
  local copies, waits for them, and re-layouts  5.46 us (17%)
  between operations  0.65 us (2%)
    pallas_call x1, Pallas kernels, whole_batch(): pl.pallas_call(functools.partial(gather_kernel, depth), out_shape=(jax.Sh...  25.2 us
    unnamed x12, local copies, waits for them, and re-layouts  4.83 us

profile of v2, /device:TPU:1, one launch (start us, length us, event | category | flops | bytes accessed | tf_op | source)
XLA Modules:
  0.0 31.3 jit_solution(3326423828813898302)
XLA Ops:
  0.6 0.0 copy-start
  0.6 0.8 %copy-done = bf16[10,1536]{1,0:T(8,128)(2,1)S(1)} copy-done((bf16[10,1536]{1,0:T(8,128)(2,1)S(1)}, bf16[10,1536]{1,0:T(8,128)(2,1)}, u32[]{:S(2)}) %copy-start) | copy-done | bytes 30744
  1.4 0.0 copy-start.1
  1.4 0.8 %copy-done.1 = bf16[10,1536]{1,0:T(8,128)(2,1)S(1)} copy-done((bf16[10,1536]{1,0:T(8,128)(2,1)S(1)}, bf16[10,1536]{1,0:T(8,128)(2,1)}, u32[]{:S(2)}) %copy-start.1) | copy-done | bytes 30744
  2.2 0.0 copy-start.2
  2.2 0.7 %copy-done.2 = s32[10]{0:T(128)S(1)} copy-done((s32[10]{0:T(128)S(1)}, s32[10]{0:T(128)}, u32[]{:S(2)}) %copy-start.2) | copy-done | bytes 64
  2.9 0.0 copy-start.3
  2.9 0.7 %copy-done.3 = s32[10]{0:T(128)S(1)} copy-done((s32[10]{0:T(128)S(1)}, s32[10]{0:T(128)}, u32[]{:S(2)}) %copy-start.3) | copy-done | bytes 64
  3.5 0.0 copy-start.4
  3.5 0.7 %copy-done.4 = s32[10]{0:T(128)S(1)} copy-done((s32[10]{0:T(128)S(1)}, s32[10]{0:T(128)}, u32[]{:S(2)}) %copy-start.4) | copy-done | bytes 64
  4.2 25.2 %shard_map.76 = (f32[32,128]{1,0:T(8,128)S(1)}, f32[10,1536]{1,0:T(8,128)S(1)}, f32[10,1536]{1,0:T(8,128)S(1)}) custom-call(bf16[10,1536]{1,0:T(8,128)(2,1)S(1)} %copy-done, bf16[10,1536]{1,0:T(8,128)(2,1)S(1)} %copy-done.1, s32[10]{0:T(128)S(1)} %copy-done.2, s32[10]{0:T(128)S(1)} %copy-done.3, s32[10]{0:T(128)S(1)} %copy-done.4), custom_call_target="tpu_custom_call" | custom-call | tf_op jit(solution)/shard_map/pallas_call | solution.py:421
  29.4 0.6 %slice_reduce_fusion = f32[10]{0:T(128)} fusion(f32[32,128]{1,0:T(8,128)S(1)} %get-tuple-element.6), kind=kLoop, calls=%fused_computation | loop fusion | bytes 80 | tf_op jit(solution)/shard_map/slice | solution.py:454
  30.0 0.6 %copy.10 = f32[10,1536]{1,0:T(8,128)} copy(f32[10,1536]{1,0:T(8,128)S(1)} %get-tuple-element.13) | data formatting | bytes 122880
  30.7 0.6 %copy.11 = f32[10,1536]{1,0:T(8,128)} copy(f32[10,1536]{1,0:T(8,128)S(1)} %get-tuple-element.14) | data formatting | bytes 122880
Async XLA Ops:
  0.6 0.8 %copy-start = (bf16[10,1536]{1,0:T(8,128)(2,1)S(1)}, bf16[10,1536]{1,0:T(8,128)(2,1)}, u32[]{:S(2)}) copy-start(bf16[10,1536]{1,0:T(8,128)(2,1)} %q_hbm.1) | copy-start | bytes 92164
  1.4 0.8 %copy-start.1 = (bf16[10,1536]{1,0:T(8,128)(2,1)S(1)}, bf16[10,1536]{1,0:T(8,128)(2,1)}, u32[]{:S(2)}) copy-start(bf16[10,1536]{1,0:T(8,128)(2,1)} %d_hbm.1) | copy-start | bytes 92164
  2.2 0.7 %copy-start.2 = (s32[10]{0:T(128)S(1)}, s32[10]{0:T(128)}, u32[]{:S(2)}) copy-start(s32[10]{0:T(128)} %pos_hbm.1) | copy-start | bytes 124
  2.9 0.7 %copy-start.3 = (s32[10]{0:T(128)S(1)}, s32[10]{0:T(128)}, u32[]{:S(2)}) copy-start(s32[10]{0:T(128)} %qs_hbm.1) | copy-start | bytes 124
  3.5 0.7 %copy-start.4 = (s32[10]{0:T(128)S(1)}, s32[10]{0:T(128)}, u32[]{:S(2)}) copy-start(s32[10]{0:T(128)} %ds_hbm.1) | copy-start | bytes 124

commit v3 on v2

--- a/solution.py
+++ b/solution.py
@@ -448,7 +448,7 @@
             pltpu.SemaphoreType.DMA((devices,)),
         ],
         compiler_params=pltpu.CompilerParams(
-            collective_id=0, has_side_effects=True, vmem_limit_bytes=40 * 1024 * 1024
+            collective_id=0, has_side_effects=True, vmem_limit_bytes=56 * 1024 * 1024
         ),
     )(query_emb, doc_emb, positive, query_source, doc_source)
     return (loss[:rows, 0], grad_query, grad_doc)

time: 31.6 us -> 30.4 us (0.962)
  local copies, waits for them, and re-layouts: 5.46 us -> 3.54 us
  Pallas kernels: 25.2 us -> 25.9 us
    unnamed x12 -> x4, local copies, waits for them, and re-layouts: 4.83 us -> 2.22 us
    pallas_call x1, Pallas kernels: 25.2 us -> 25.9 us  [whole_batch(): pl.pallas_call(functools.partial(gather_kernel, depth), out_shape=(jax.Sh...]
    slice x1, local copies, waits for them, and re-layouts: 0.63 us -> 1.32 us  [whole_batch(): return (loss[:rows, 0], grad_query, grad_doc)]
where the time goes in v3:
time: 30.4 us; the launch traced here: 30.1 us
  Pallas kernels  25.9 us (85%)
  local copies, waits for them, and re-layouts  3.54 us (12%)
  between operations  0.64 us (2%)
    pallas_call x1, Pallas kernels, whole_batch(): pl.pallas_call(functools.partial(gather_kernel, depth), out_shape=(jax.Sh...  25.9 us
    unnamed x4, local copies, waits for them, and re-layouts  2.22 us
    slice x1, local copies, waits for them, and re-layouts, whole_batch(): return (loss[:rows, 0], grad_query, grad_doc)  1.32 us

profile of v3, /device:TPU:1, one launch (start us, length us, event | category | flops | bytes accessed | tf_op | source)
XLA Modules:
  0.0 30.1 jit_solution(7318387914692356669)
XLA Ops:
  0.6 25.9 %shard_map.76 = (f32[32,128]{1,0:T(8,128)}, f32[10,1536]{1,0:T(8,128)}, f32[10,1536]{1,0:T(8,128)}) custom-call(bf16[10,1536]{1,0:T(8,128)(2,1)} %q_hbm.1, bf16[10,1536]{1,0:T(8,128)(2,1)} %d_hbm.1, s32[10]{0:T(128)} %pos_hbm.1, s32[10]{0:T(128)} %qs_hbm.1, s32[10]{0:T(128)} %ds_hbm.1), custom_call_target="tpu_custom_call" | custom-call | tf_op jit(solution)/shard_map/pallas_call | solution.py:421
  26.6 1.3 %slice_reduce_fusion = f32[10]{0:T(128)} fusion(f32[32,128]{1,0:T(8,128)} %get-tuple-element.6), kind=kLoop, calls=%fused_computation | loop fusion | bytes 80 | tf_op jit(solution)/shard_map/slice | solution.py:454
  27.9 0.0 copy-start
  27.9 1.6 %copy.10 = f32[10,1536]{1,0:T(8,128)} copy(f32[10,1536]{1,0:T(8,128)} %get-tuple-element.13) | data formatting | bytes 122880
  29.5 0.0 copy-done
  29.5 0.6 %copy.11 = f32[10,1536]{1,0:T(8,128)} copy(f32[10,1536]{1,0:T(8,128)S(1)} %copy-done) | data formatting | bytes 122880
Async XLA Ops:
  27.9 1.6 %copy-start = (f32[10,1536]{1,0:T(8,128)S(1)}, f32[10,1536]{1,0:T(8,128)}, u32[]{:S(2)}) copy-start(f32[10,1536]{1,0:T(8,128)} %get-tuple-element.14) | copy-start | bytes 184324

commit v4 on v3

--- a/solution.py
+++ b/solution.py
@@ -194,7 +194,7 @@
 
 
 def gather_kernel(
-    depth, q_hbm, d_hbm, pos_hbm, qs_hbm, ds_hbm, loss_ref, gq_ref, gd_ref,
+    depth, q_hbm, d_hbm, pos_hbm, qs_hbm, ds_hbm, out_ref,
     q_ref, d_ref, pos_ref, qs_ref, ds_ref, in_sem, buf, rows_all, unit_own, len_own, scol, ucol, srow, urow, lse_self, lse_pair, send_sem, recv_sem,
 ):
     f32, bf16 = jnp.float32, jnp.bfloat16
@@ -354,7 +354,8 @@
         select((tails, heads), lambda r, c, k=k: c == r // 4 * 16 + k * 4 + r % 4) for k in range(4)
     ]
     for k in range(4):
-        rows_all[heads:, k * quarter : (k + 1) * quarter] = mm(picks[k], left).astype(bf16)
+        rows_all[heads:count, k * quarter : (k + 1) * quarter] = mm(picks[k], left).astype(bf16)
+    rows_all[count:, :] = own
     meta_tail = mm(picks[0], meta).astype(bf16)
 
     def reader(first, axis, shape):
@@ -368,45 +369,32 @@
         ref[:, 0:heads] = mmt(reader(first, 1, (8, 128)), meta)
         ref[:, heads:] = mmt(reader(first + 4, 1, (8, 128)), meta_tail)
     s_row, u_row = srow[0:1, :], urow[0:1, :]
-    lse_self[...] = jnp.zeros_like(lse_self)
-    lse_pair[...] = jnp.zeros_like(lse_pair)
-    chunk = count
-
-    def forward(step, carry):
-        at = pl.ds(pl.multiple_of(step * chunk, chunk), chunk)
-        scores = mmt(rows_all[at, :], rows_all[...]) * INV_TAU
-        apart = u_row - ucol[at, 0:1]
-        allowed = (apart == 0.25) | ((s_row != scol[at, 0:1]) & (apart != -0.25))
-        scores = jnp.where(allowed, scores, NEG)
-        peak = jnp.max(scores, axis=1, keepdims=True)
-        total = jnp.sum(jnp.exp(scores - peak), axis=1, keepdims=True)
-        lse = jnp.where(peak > 0.5 * NEG, peak + jnp.log(total), NEG)
-        lse_self[0:1, :] += jnp.sum(jnp.where(apart == 0.0, lse, 0.0), axis=0, keepdims=True)
-        lse_pair[0:1, :] += jnp.sum(
-            jnp.where(jnp.abs(apart) == 0.25, lse, 0.0), axis=0, keepdims=True
-        )
-        return carry
-
-    lax.fori_loop(0, count // chunk, forward, 0)
-    first, second = lse_self[0:1, :], lse_pair[0:1, :]
+    everything = mmt(rows_all[...], rows_all[0:count, :]) * INV_TAU
+    apart = u_row - ucol[:, 0:1]
+    allowed = (apart == 0.25) | ((s_row != scol[:, 0:1]) & (apart != -0.25))
+    scores = jnp.where(allowed, everything[0:count, :], NEG)
+    peak = jnp.max(scores, axis=1, keepdims=True)
+    total = jnp.sum(jnp.exp(scores - peak), axis=1, keepdims=True)
+    lse = jnp.where(peak > 0.5 * NEG, peak + jnp.log(total), NEG)
+    first = jnp.sum(jnp.where(apart == 0.0, lse, 0.0), axis=0, keepdims=True)
+    second = jnp.sum(jnp.where(jnp.abs(apart) == 0.25, lse, 0.0), axis=0, keepdims=True)
     norm_row = jnp.maximum(first, second) + jnp.log(1.0 + jnp.exp(-jnp.abs(first - second)))
 
-    scores = mmt(own, rows_all[...]) * INV_TAU
+    scores = everything[count:, :]
     apart = u_row - own_key[:, 0:1]
     hit = jnp.abs(apart) == 0.25
     norm_own = jnp.sum(jnp.where(apart == 0.0, norm_row, 0.0), axis=1, keepdims=True)
     loss = norm_own - jnp.sum(jnp.where(hit, scores, 0.0), axis=1, keepdims=True)
-    loss_ref[...] = jnp.broadcast_to(loss, loss_ref.shape)
+    out_ref[:, width:] = jnp.broadcast_to(loss, (32, 128))
     from_own = jnp.exp(scores - norm_own)
     apart_source = (s_row != own_source[:, 0:1]) & (own_key[:, 0:1] >= 0.0)
     weights = jnp.where(
         hit, from_own - 1.0, jnp.where(apart_source, from_own + jnp.exp(scores - norm_row), 0.0)
     )
-    grads = mm(weights.astype(bf16), rows_all[...]) * INV_TAU
+    grads = mm(weights.astype(bf16), rows_all[0:count, :]) * INV_TAU
     unit = unit_own[...]
     grads = (grads - unit * jnp.sum(unit * grads, axis=1, keepdims=True)) / len_own[:, 0:1]
-    gq_ref[...] = grads[0:rows, :]
-    gd_ref[...] = grads[16 : 16 + rows, :]
+    out_ref[:, 0:width] = grads
 
     for one in started:
         one.wait_send()
@@ -418,15 +406,11 @@
     count = 2 * rows * devices
     vmem = pl.BlockSpec(memory_space=pltpu.VMEM)
     f32 = jnp.float32
-    loss, grad_query, grad_doc = pl.pallas_call(
+    out = pl.pallas_call(
         functools.partial(gather_kernel, depth),
-        out_shape=(
-            jax.ShapeDtypeStruct((32, 128), f32),
-            jax.ShapeDtypeStruct((rows, width), f32),
-            jax.ShapeDtypeStruct((rows, width), f32),
-        ),
+        out_shape=jax.ShapeDtypeStruct((32, width + 128), f32),
         in_specs=[pl.BlockSpec(memory_space=pltpu.HBM)] * 5,
-        out_specs=(vmem, vmem, vmem),
+        out_specs=vmem,
         scratch_shapes=[
             pltpu.VMEM((rows, width), jnp.bfloat16),
             pltpu.VMEM((rows, width), jnp.bfloat16),
@@ -435,7 +419,7 @@
             pltpu.SMEM((rows,), jnp.int32),
             pltpu.SemaphoreType.DMA((5,)),
             pltpu.VMEM((devices * 16, width + width // 4 + 128), jnp.bfloat16),
-            pltpu.VMEM((count, width), jnp.bfloat16),
+            pltpu.VMEM((count + 32, width), jnp.bfloat16),
             pltpu.VMEM((32, width), f32),
             pltpu.VMEM((32, 128), f32),
             pltpu.VMEM((count, 128), f32),
@@ -451,7 +435,7 @@
             collective_id=0, has_side_effects=True, vmem_limit_bytes=56 * 1024 * 1024
         ),
     )(query_emb, doc_emb, positive, query_source, doc_source)
-    return (loss[:rows, 0], grad_query, grad_doc)
+    return (out[:rows, width], out[:rows, :width], out[16 : 16 + rows, :width])
 
 
 def solution(mesh):

time: 30.4 us -> 29.7 us (0.977)
  local copies, waits for them, and re-layouts: 3.54 us -> 2.95 us
    unnamed x4 -> x0, local copies, waits for them, and re-layouts: 2.22 us -> none
    slice x1 -> x2, local copies, waits for them, and re-layouts: 1.32 us -> 2.95 us  [whole_batch(): return (out[:rows, width], out[:rows, :width], out[16:16 + rows, :width])]
where the time goes in v4:
time: 29.7 us; the launch traced here: 29.4 us
  Pallas kernels  25.8 us (87%)
  local copies, waits for them, and re-layouts  2.95 us (10%)
  between operations  0.64 us (2%)
    pallas_call x1, Pallas kernels, whole_batch(): pl.pallas_call(functools.partial(gather_kernel, depth), out_shape=jax.Sha...  25.8 us
    slice x2, local copies, waits for them, and re-layouts, whole_batch(): return (out[:rows, width], out[:rows, :width], out[16:16 + rows, :width])  2.95 us

profile of v4, /device:TPU:1, one launch (start us, length us, event | category | flops | bytes accessed | tf_op | source)
XLA Modules:
  0.0 29.4 jit_solution(5090544455855011434)
XLA Ops:
  0.6 25.8 %shard_map.76 = f32[32,1664]{1,0:T(8,128)} custom-call(bf16[10,1536]{1,0:T(8,128)(2,1)} %q_hbm.1, bf16[10,1536]{1,0:T(8,128)(2,1)} %d_hbm.1, s32[10]{0:T(128)} %pos_hbm.1, s32[10]{0:T(128)} %qs_hbm.1, s32[10]{0:T(128)} %ds_hbm.1), custom_call_target="tpu_custom_call" | custom-call | tf_op jit(solution)/shard_map/pallas_call | solution.py:409
  26.5 1.6 %fusion = (f32[10,1536]{1,0:T(8,128)}, f32[10,1536]{1,0:T(8,128)}) fusion(f32[32,1664]{1,0:T(8,128)} %shard_map.76), kind=kLoop, calls=%fused_computation.1 | loop fusion | bytes 245760 | tf_op jit(solution)/shard_map/slice | solution.py:438
  28.1 1.3 %slice_reduce_fusion = f32[10]{0:T(128)} fusion(f32[32,1664]{1,0:T(8,128)} %shard_map.76), kind=kLoop, calls=%fused_computation | loop fusion | bytes 80 | tf_op jit(solution)/shard_map/slice | solution.py:438

commit v5 on v4

--- a/solution.py
+++ b/solution.py
@@ -342,12 +342,18 @@
                 arrive(s + 1 - 2 * core)
         return carry
 
+    def place_rows(pair, which):
+        at = pl.ds(pl.multiple_of((2 * pair + which) * 16, 16), 16)
+        rows_all[at, :] = buf[at, 0:width]
+        return which
+
+    lax.fori_loop(0, buf.shape[0] // 32, place_rows, core)
     lax.fori_loop(0, depth, from_core, 0)
+    lax.fori_loop(0, buf.shape[0] // 32, place_rows, 1 - core)
 
     count = 2 * rows * buf.shape[0] // 16
     heads = buf.shape[0]
     tails = count - heads
-    rows_all[0:heads, :] = buf[:, 0:width]
     left = buf[:, width : width + quarter]
     meta = buf[:, width + quarter :]
     picks = [

time: 29.7 us -> 29.8 us (level)
  no operation moved by 1% of the time
where the time goes in v5:
time: 29.8 us; the launch traced here: 29.5 us
  Pallas kernels  25.9 us (87%)
  local copies, waits for them, and re-layouts  2.95 us (10%)
  between operations  0.64 us (2%)
    pallas_call x1, Pallas kernels, whole_batch(): pl.pallas_call(functools.partial(gather_kernel, depth), out_shape=jax.Sha...  25.9 us
    slice x2, local copies, waits for them, and re-layouts, whole_batch(): return (out[:rows, width], out[:rows, :width], out[16:16 + rows, :width])  2.95 us

profile of v5, /device:TPU:1, one launch (start us, length us, event | category | flops | bytes accessed | tf_op | source)
XLA Modules:
  0.0 29.5 jit_solution(6725743154766741494)
XLA Ops:
  0.6 25.9 %shard_map.76 = f32[32,1664]{1,0:T(8,128)} custom-call(bf16[10,1536]{1,0:T(8,128)(2,1)} %q_hbm.1, bf16[10,1536]{1,0:T(8,128)(2,1)} %d_hbm.1, s32[10]{0:T(128)} %pos_hbm.1, s32[10]{0:T(128)} %qs_hbm.1, s32[10]{0:T(128)} %ds_hbm.1), custom_call_target="tpu_custom_call" | custom-call | tf_op jit(solution)/shard_map/pallas_call | solution.py:415
  26.6 1.6 %fusion = (f32[10,1536]{1,0:T(8,128)}, f32[10,1536]{1,0:T(8,128)}) fusion(f32[32,1664]{1,0:T(8,128)} %shard_map.76), kind=kLoop, calls=%fused_computation.1 | loop fusion | bytes 245760 | tf_op jit(solution)/shard_map/slice | solution.py:444
  28.2 1.3 %slice_reduce_fusion = f32[10]{0:T(128)} fusion(f32[32,1664]{1,0:T(8,128)} %shard_map.76), kind=kLoop, calls=%fused_computation | loop fusion | bytes 80 | tf_op jit(solution)/shard_map/slice | solution.py:444
